TPU v7x, 128 devices: a whole 4x4x4 slice. The times are simulated.
128 devices in a mesh: grp: 8 (over y, z_hi), lm: 16 (over x, z_lo, core).
Axes of the slice: x: 4, y: 4, z: 4 (z_hi: 2, z_lo: 2; z = z_hi * 2 + z_lo), core: 2. Of those that a mesh axis runs over, the one named last changes fastest.
Arguments:
- embeddings: bfloat16 [32768, 512], P(('grp', 'lm')), may hold values from -14 to 14
- landmarks: bfloat16 [32768, 512], P('lm'), may hold values from -14 to 14
- start_vectors: float32 [32768, 128], P(('grp', 'lm')), may hold values from -10 to 10
- row_weight: float32 [32768], P(('grp', 'lm')), may hold values from 0.1 to 9
- spread: float32 [1], replicated, may hold values from 11.313708 to 33.941124
Outputs:
- subspace: float32 [32768, 128], P(('grp', 'lm'))
All inputs are finite; a program needn't handle non-finite values.
Results may differ from a plain program's by a relative error of at most 0.019.
Values may be sent and summed in bfloat16 or wider, within the bound.
No kernel may reach another device: no remote copies, remote signals or barrier semaphores. Data moves between devices by JAX's collectives and lax.ppermute only.
A program may use at most 128 MiB of HBM per device.

v0:
```python
import jax
import jax.numpy as jnp
from jax import lax
from jax.sharding import PartitionSpec as P

ITERS = 2


def unit_rows(values):
    values = values.astype(jnp.float32)
    scale = lax.rsqrt(jnp.sum(values * values, axis=1, keepdims=True) + 1e-06)
    return (values * scale).astype(jnp.bfloat16)


def kernel_values(rows_unit, marks_unit, gamma):
    cosine = jnp.einsum("rd,ld->rl", rows_unit, marks_unit, preferred_element_type=jnp.float32)
    return jnp.exp(gamma * cosine)


def local(embeddings, landmarks, start_vectors, row_weight, spread):
    own_rows = embeddings.shape[0]
    marks = landmarks.shape[0]
    groups = lax.axis_size("grp")
    members = lax.axis_size("lm")
    total_rows = own_rows * groups * members
    group_rows = own_rows * members
    gamma = spread[0]
    rows_unit = unit_rows(embeddings)
    marks_unit = unit_rows(landmarks)
    sums = jnp.zeros((marks,), jnp.float32)
    weights = jnp.zeros((group_rows,), jnp.float32)
    part_rows = lax.all_gather(rows_unit, "lm", axis=0, tiled=True)
    part_weight = lax.all_gather(row_weight.astype(jnp.bfloat16), "lm", axis=0, tiled=True).astype(
        jnp.float32
    )
    values = kernel_values(part_rows, marks_unit, gamma)
    build_tile = values.astype(jnp.bfloat16)
    weights = lax.dynamic_update_slice_in_dim(weights, part_weight, jnp.int32(0), 0)
    sums = sums + jnp.sum(part_weight[:, None] * values, axis=0)
    mean_sum, weight_sum = lax.psum((sums, jnp.sum(weights)), "grp")
    means = mean_sum / weight_sum
    vectors = start_vectors
    weighted_full = row_weight[:, None] * vectors
    totals = lax.psum(jnp.sum(weighted_full, axis=0), ("grp", "lm"))
    group_weighted = lax.all_gather(weighted_full.astype(jnp.bfloat16), "lm", axis=0, tiled=True)
    for step in range(ITERS):
        side = (
            lax.psum(
                jnp.einsum(
                    "rl,rv->lv", build_tile, group_weighted, preferred_element_type=jnp.float32
                ),
                "grp",
            )
            - means[:, None] * totals[None, :]
        )
        side_b = side.astype(jnp.bfloat16)
        shift = jnp.dot(means, side_b.astype(jnp.float32), precision=lax.Precision.HIGHEST)
        image = lax.psum_scatter(
            weights[:, None]
            * (jnp.dot(build_tile, side_b, preferred_element_type=jnp.float32) - shift[None, :]),
            "lm",
            scatter_dimension=0,
            tiled=True,
        )
        square, column = lax.psum(
            (jnp.sum(image * image, axis=0), jnp.sum(row_weight[:, None] * image, axis=0)),
            ("grp", "lm"),
        )
        scale = jnp.sqrt(square / total_rows + 1e-06)
        vectors = image / scale[None, :]
        totals = column / scale
        if step + 1 < ITERS:
            group_weighted = lax.all_gather(
                (row_weight[:, None] * vectors).astype(jnp.bfloat16), "lm", axis=0, tiled=True
            )
    return vectors


def solution(mesh):
    in_specs = (
        P(("grp", "lm"), None),
        P("lm", None),
        P(("grp", "lm"), None),
        P(("grp", "lm")),
        P(),
    )
    out_specs = P(("grp", "lm"), None)
    return jax.shard_map(local, mesh=mesh, in_specs=in_specs, out_specs=out_specs, check_vma=False)
```

profile of v0, /device:TPU:1, one launch (start us, length us, event | category | flops | bytes accessed | tf_op | source)
XLA Modules:
  0.0 612.0 jit_solution(1574066524591326856)
XLA Ops:
  6.5 1.1 fusion.8
  7.6 1.8 fusion.9
  9.5 1.6 multiply_reduce_fusion.4
  11.2 2.1 fusion.3
  14.0 21.3 %all-gather = bf16[16,1,256]{2,1,0:T(2,128)(2,1)S(1)} all-gather(bf16[1,1,256]{2,1,0:T(2,128)(2,1)S(1)} %reshape.21), channel_id=1, replica_groups=mesh['grp'=8,'lm'=16] {'lm'}, dimensions={0}, use_global_device_ids=true | all-gather | bytes 8704 | tf_op jit(solution)/shard_map/all_gather | solution.py:33
  36.0 14.6 %all-gather.5.cloned.1.call-done = bf16[4096,512]{1,0:T(8,128)(2,1)} async-done(((bf16[256,512]{1,0:T(8,128)(2,1)}), bf16[4096,512]{1,0:T(8,128)(2,1)}) %all-gather.5.cloned.1.call-update) | async-done | bytes 4194320 | tf_op jit(solution)/shard_map/all_gather | solution.py:32
  50.6 16.2 %multiply_reduce_fusion = (f32[2048]{0:T(1024)S(1)}, bf16[4096,2048]{1,0:T(8,128)(2,1)}) fusion(f32[4096]{0:T(1024)S(1)} %bitcast.20, f32[]{:T(128)} %bitcast.17, bf16[4096,512]{1,0:T(8,128)(2,1)} %all-gather.5.cloned.1.call-done, bf16[2048,512]{1,0:T(8,128)(2,1)} %param.6, f32[2048]{0:T(1024)S(1)} %add_rsqrt_fusion), kind=kOutput, calls=%fused_computation | convolution fusion | flops 8626632704 | bytes 23101444 | tf_op jit(solution)/shard_map/rd,ld->rl/dot_general | solution.py:16
  66.7 18.1 %all-gather.7.cloned.1.call-done = bf16[4096,128]{1,0:T(8,128)(2,1)} async-done(((bf16[256,128]{1,0:T(8,128)(2,1)}), bf16[4096,128]{1,0:T(8,128)(2,1)}) %all-gather.7.cloned.1.call-update) | async-done | bytes 1048592 | tf_op jit(solution)/shard_map/all_gather | solution.py:45
  84.8 11.6 %fusion.11 = f32[2048,128]{1,0:T(8,128)} fusion(bf16[4096,2048]{1,0:T(8,128)(2,1)} %get-tuple-element.12, bf16[4096,128]{1,0:T(8,128)(2,1)} %all-gather.7.cloned.1.call-done), kind=kOutput, calls=%fused_computation.35 | convolution fusion | flops 2147483648 | bytes 18874368 | tf_op jit(solution)/shard_map/rl,rv->lv/dot_general | solution.py:49
  96.5 69.1 %psum.59 = f32[128]{0:T(128)S(1)} all-reduce(f32[128]{0:T(128)S(1)} %get-tuple-element.13), channel_id=1, replica_groups=mesh['grp'=8,'lm'=16] {'grp','lm'}, use_global_device_ids=true, to_apply=%region_8.0 | all-reduce | flops 128 | bytes 1024 | tf_op jit(solution)/shard_map/psum | solution.py:44
  166.3 19.9 %all-reduce.1 = (f32[2048]{0:T(1024)S(1)}, f32[]{:T(128)}) all-reduce(f32[2048]{0:T(1024)S(1)} %get-tuple-element.11, f32[]{:T(128)} %convert_reduce_fusion), channel_id=1, replica_groups=mesh['grp'=8,'lm'=16] {'grp'}, use_global_device_ids=true, to_apply=%region_4.0 | all-reduce | flops 2049 | bytes 16392 | tf_op jit(solution)/shard_map/psum | solution.py:40
  186.9 1.8 convolution_bitcast_fusion.1
  188.7 12.0 %fusion.2 = f32[4096,128]{1,0:T(8,128)} fusion(bf16[4096,2048]{1,0:T(8,128)(2,1)} %get-tuple-element.12, f32[128]{0:T(128)S(1)} %convolution_bitcast_fusion.1, f32[4096]{0:T(1024)S(1)} %bitcast.21, f32[2048,128]{1,0:T(8,128)} %all-reduce.5.cloned.1.call-done, f32[128]{0:T(128)S(1)} %psum.59, f32[2048]{0:T(1024)S(1)} %broadcast_divide_fusion.1), kind=kOutput, calls=%fused_computation.8 | convolution fusion | flops 2149318656 | bytes 19948544 | tf_op jit(solution)/shard_map/dot_general | solution.py:60
  200.7 61.7 %reduce-scatter.3.cloned.1.call-done = f32[256,128]{1,0:T(8,128)} async-done(((f32[4096,128]{1,0:T(8,128)}), f32[256,128]{1,0:T(8,128)}) %reduce-scatter.3.cloned.1.call-update) | async-done | bytes 131088 | tf_op jit(solution)/shard_map/reduce_scatter | solution.py:58
  263.5 67.6 %all-reduce = (f32[128]{0:T(128)S(1)}, f32[128]{0:T(128)S(1)}) all-reduce(f32[128]{0:T(128)S(1)} %get-tuple-element.6, f32[128]{0:T(128)S(1)} %get-tuple-element.5), channel_id=1, replica_groups=mesh['grp'=8,'lm'=16] {'grp','lm'}, use_global_device_ids=true, to_apply=%region_11.0 | all-reduce | flops 256 | bytes 2048 | tf_op jit(solution)/shard_map/psum | solution.py:65
  331.1 1.6 multiply_convert_fusion
  333.1 29.2 %all-gather.9.cloned.1.call-done = bf16[4096,128]{1,0:T(8,128)(2,1)} async-done(((bf16[256,128]{1,0:T(8,128)(2,1)}), bf16[4096,128]{1,0:T(8,128)(2,1)}) %all-gather.9.cloned.1.call-update) | async-done | bytes 1048592 | tf_op jit(solution)/shard_map/all_gather | solution.py:73
  362.2 11.6 %fusion.12 = f32[2048,128]{1,0:T(8,128)} fusion(bf16[4096,2048]{1,0:T(8,128)(2,1)} %get-tuple-element.12, bf16[4096,128]{1,0:T(8,128)(2,1)} %all-gather.9.cloned.1.call-done), kind=kOutput, calls=%fused_computation.36 | convolution fusion | flops 2147483648 | bytes 18874368 | tf_op jit(solution)/shard_map/rl,rv->lv/dot_general | solution.py:49
  373.9 83.7 %all-reduce.7.cloned.1.call-done = f32[2048,128]{1,0:T(8,128)} async-done(((f32[2048,128]{1,0:T(8,128)}), f32[2048,128]{1,0:T(8,128)}) %all-reduce.7.cloned.1.call-update) | async-done | bytes 1048592 | tf_op jit(solution)/shard_map/psum | solution.py:48
  457.6 1.8 convolution_bitcast_fusion
  459.4 12.0 %fusion.1 = f32[4096,128]{1,0:T(8,128)} fusion(bf16[4096,2048]{1,0:T(8,128)(2,1)} %get-tuple-element.12, f32[128]{0:T(128)S(1)} %convolution_bitcast_fusion, f32[4096]{0:T(1024)S(1)} %bitcast.22, f32[2048,128]{1,0:T(8,128)} %all-reduce.7.cloned.1.call-done, f32[128]{0:T(128)S(1)} %get-tuple-element.15, f32[2048]{0:T(1024)S(1)} %broadcast_divide_fusion.1), kind=kOutput, calls=%fused_computation.6 | convolution fusion | flops 2149318656 | bytes 19948544 | tf_op jit(solution)/shard_map/dot_general | solution.py:60
  471.4 63.1 %reduce-scatter.5.cloned.1.call-done = f32[256,128]{1,0:T(8,128)} async-done(((f32[4096,128]{1,0:T(8,128)}), f32[256,128]{1,0:T(8,128)}) %reduce-scatter.5.cloned.1.call-update) | async-done | bytes 131088 | tf_op jit(solution)/shard_map/reduce_scatter | solution.py:58
  535.4 68.2 %psum.63 = f32[128]{0:T(128)S(1)} all-reduce(f32[128]{0:T(128)S(1)} %multiply_reduce_fusion.1), channel_id=1, replica_groups=mesh['grp'=8,'lm'=16] {'grp','lm'}, use_global_device_ids=true, to_apply=%region_17.0 | all-reduce | flops 128 | bytes 1024 | tf_op jit(solution)/shard_map/psum | solution.py:65
  603.6 1.6 broadcast_divide_fusion
  (28 shorter events, 4.6 us)
Async XLA Ops:
  6.5 44.0 %all-gather.5.cloned.1.call-start = ((), (), s32[]{:S(2)}) async-start(), calls=%async_computation.2 | async-start | bytes 4456448 | tf_op jit(solution)/shard_map/all_gather | solution.py:32
  9.4 75.4 %all-gather.7.cloned.1.call-start = ((), (), s32[]{:S(2)}) async-start(), calls=%async_computation.3 | async-start | bytes 1114112 | tf_op jit(solution)/shard_map/all_gather | solution.py:45
  11.1 175.7 %all-reduce.5.cloned.1.call-start = ((), (), s32[]{:S(2)}) async-start(), calls=%async_computation.4 | async-start | bytes 2097152 | tf_op jit(solution)/shard_map/psum | solution.py:48
  96.5 166.0 %reduce-scatter.3.cloned.1.call-start = ((), (), s32[]{:S(2)}) async-start(), calls=%async_computation.5 | async-start | bytes 2228224 | tf_op jit(solution)/shard_map/reduce_scatter | solution.py:58
  188.7 73.8 %copy-start = (f32[256]{0:T(256)S(1)}, f32[256]{0:T(256)}, u32[]{:S(2)}) copy-start(f32[256]{0:T(256)} %param.8) | copy-start | bytes 3076
  200.7 161.5 %all-gather.9.cloned.1.call-start = ((), (), s32[]{:S(2)}) async-start(), calls=%async_computation.6 | async-start | bytes 1114112 | tf_op jit(solution)/shard_map/all_gather | solution.py:73
  332.8 124.8 %all-reduce.7.cloned.1.call-start = ((), (), s32[]{:S(2)}) async-start(), calls=%async_computation.7 | async-start | bytes 2097152 | tf_op jit(solution)/shard_map/psum | solution.py:48
  373.9 160.6 %reduce-scatter.5.cloned.1.call-start = ((), (), s32[]{:S(2)}) async-start(), calls=%async_computation.8 | async-start | bytes 2228224 | tf_op jit(solution)/shard_map/reduce_scatter | solution.py:58
Sparse Core Ops, SparseCore 0:
  9.5 40.9 all-gather.4
  52.3 32.5 all-gather.6
  96.6 84.5 all-reduce.4
  200.8 61.5 reduce-scatter.2
  332.9 29.2 all-gather.8
  374.0 83.5 all-reduce.6
  471.5 62.8 reduce-scatter.4
where the time goes:
time: 613 us; the launch traced here: 612 us
  waiting for transfers between devices  270 us (44%)
  blocking collectives  246 us (40%)
  matrix products  67 us (11%)
  between operations  14.2 us (2%)
  other arithmetic  13.8 us (2%)
    psum x2, blocking collectives, local(): lax.psum((jnp.sum(image * image, axis=0), jnp.sum(row_weight[:, None] * i...  136 us
    reduce_scatter x2, waiting for transfers between devices, local(): lax.psum_scatter(weights[:, None] * (jnp.dot(build_tile, side_b, preferre...  125 us
    psum x2, waiting for transfers between devices, local(): lax.psum(jnp.einsum('rl,rv->lv', build_tile, group_weighted, preferred_el...  83.7 us
    psum x1, blocking collectives, local(): totals = lax.psum(jnp.sum(weighted_full, axis=0), ('grp', 'lm'))  69.1 us
    all_gather x1, waiting for transfers between devices, local(): lax.all_gather((row_weight[:, None] * vectors).astype(jnp.bfloat16), 'lm'...  29.2 us
    dot_general x2, matrix products, local(): jnp.dot(build_tile, side_b, preferred_element_type=jnp.float32)  24 us
    dot_general x2, matrix products, local(): jnp.einsum('rl,rv->lv', build_tile, group_weighted, preferred_element_typ...  23.2 us
    all_gather x1, blocking collectives, local(): lax.all_gather(row_weight.astype(jnp.bfloat16), 'lm', axis=0, tiled=True)  21.3 us
  transfers between devices with their start and end apart: 7, of which 6 were waited for; matrix products, arithmetic and copies ran while one was open for 4% of the time, Pallas kernels for 0%

commit v1 on v0

--- a/solution.py
+++ b/solution.py
@@ -4,6 +4,11 @@
 from jax.sharding import PartitionSpec as P
 
 ITERS = 2
+
+
+def summed_here(block, mesh_axis):
+    terms = lax.all_gather(block, mesh_axis)
+    return jnp.sum(terms, axis=0)
 
 
 def unit_rows(values):
@@ -45,7 +50,7 @@
     group_weighted = lax.all_gather(weighted_full.astype(jnp.bfloat16), "lm", axis=0, tiled=True)
     for step in range(ITERS):
         side = (
-            lax.psum(
+            summed_here(
                 jnp.einsum(
                     "rl,rv->lv", build_tile, group_weighted, preferred_element_type=jnp.float32
                 ),

time: 613 us -> 665 us (1.085)
  blocking collectives: 246 us -> 274 us
  waiting for transfers between devices: 270 us -> 291 us
  other arithmetic: 13.8 us -> 21.6 us
    all_gather x0 -> x2, waiting for transfers between devices: none -> 108 us  [summed_here(): terms = lax.all_gather(block, mesh_axis)]
    psum x2 -> x0, waiting for transfers between devices: 83.7 us -> none  [local(): lax.psum(jnp.einsum('rl,rv->lv', build_tile, group_weighted, preferred_el...]
    psum x1, blocking collectives: 69.1 us -> 98.7 us  [local(): totals = lax.psum(jnp.sum(weighted_full, axis=0), ('grp', 'lm'))]
    reduce_sum x0 -> x2, other arithmetic: none -> 7.8 us  [summed_here(): return jnp.sum(terms, axis=0)]
  transfers between devices with their start and end apart: 7 -> 7, of which waited for: 6 -> 6; matrix products, arithmetic and copies ran while one was open for 4% -> 3% of each run, Pallas kernels for 0% -> 0%
where the time goes in v1:
time: 665 us
  waiting for transfers between devices  291 us (44%)
  blocking collectives  274 us (41%)
  matrix products  64.2 us (10%)
  other arithmetic  21.6 us (3%)
  between operations  14.2 us (2%)
    psum x2, blocking collectives, local(): lax.psum((jnp.sum(image * image, axis=0), jnp.sum(row_weight[:, None] * i...  136 us
    reduce_scatter x2, waiting for transfers between devices, local(): lax.psum_scatter(weights[:, None] * (jnp.dot(build_tile, side_b, preferre...  120 us
    all_gather x2, waiting for transfers between devices, summed_here(): terms = lax.all_gather(block, mesh_axis)  108 us
    psum x1, blocking collectives, local(): totals = lax.psum(jnp.sum(weighted_full, axis=0), ('grp', 'lm'))  98.7 us
    all_gather x1, waiting for transfers between devices, local(): lax.all_gather((row_weight[:, None] * vectors).astype(jnp.bfloat16), 'lm'...  29.2 us
    dot_general x2, matrix products, local(): jnp.dot(build_tile, side_b, preferred_element_type=jnp.float32)  23.6 us
    dot_general x2, matrix products, local(): jnp.einsum('rl,rv->lv', build_tile, group_weighted, preferred_element_typ...  23.4 us
    all_gather x1, blocking collectives, local(): lax.all_gather(row_weight.astype(jnp.bfloat16), 'lm', axis=0, tiled=True)  21.4 us
  transfers between devices with their start and end apart: 7, of which 6 were waited for; matrix products, arithmetic and copies ran while one was open for 3% of the time, Pallas kernels for 0%

profile of v1, /device:TPU:1, one launch (start us, length us, event | category | flops | bytes accessed | tf_op | source)
XLA Modules:
  0.0 664.8 jit_solution(5445728159958721024)
XLA Ops:
  6.5 1.1 fusion.8
  7.6 1.8 fusion.9
  9.5 1.6 multiply_reduce_fusion.4
  11.2 2.1 fusion.3
  14.6 21.4 %all-gather.2 = bf16[16,1,256]{2,1,0:T(2,128)(2,1)S(1)} all-gather(bf16[1,1,256]{2,1,0:T(2,128)(2,1)S(1)} %reshape.23), channel_id=1, replica_groups=mesh['grp'=8,'lm'=16] {'lm'}, dimensions={0}, use_global_device_ids=true | all-gather | bytes 8704 | tf_op jit(solution)/shard_map/all_gather | solution.py:38
  36.0 14.6 %all-gather.9.cloned.1.call-done = bf16[4096,512]{1,0:T(8,128)(2,1)} async-done(((bf16[256,512]{1,0:T(8,128)(2,1)}), bf16[4096,512]{1,0:T(8,128)(2,1)}) %all-gather.9.cloned.1.call-update) | async-done | bytes 4194320 | tf_op jit(solution)/shard_map/all_gather | solution.py:37
  50.6 16.2 %multiply_reduce_fusion = (f32[2048]{0:T(1024)S(1)}, bf16[4096,2048]{1,0:T(8,128)(2,1)}) fusion(f32[4096]{0:T(1024)S(1)} %bitcast.24, f32[]{:T(128)} %bitcast.19, bf16[4096,512]{1,0:T(8,128)(2,1)} %all-gather.9.cloned.1.call-done, bf16[2048,512]{1,0:T(8,128)(2,1)} %param.6, f32[2048]{0:T(1024)S(1)} %add_rsqrt_fusion), kind=kOutput, calls=%fused_computation | convolution fusion | flops 8626632704 | bytes 23101444 | tf_op jit(solution)/shard_map/rd,ld->rl/dot_general | solution.py:21
  66.8 18.0 %all-gather.11.cloned.1.call-done = bf16[4096,128]{1,0:T(8,128)(2,1)} async-done(((bf16[256,128]{1,0:T(8,128)(2,1)}), bf16[4096,128]{1,0:T(8,128)(2,1)}) %all-gather.11.cloned.1.call-update) | async-done | bytes 1048592 | tf_op jit(solution)/shard_map/all_gather | solution.py:50
  84.8 11.7 %fusion.11 = f32[2048,128]{1,0:T(8,128)} fusion(bf16[4096,2048]{1,0:T(8,128)(2,1)} %get-tuple-element.12, bf16[4096,128]{1,0:T(8,128)(2,1)} %all-gather.11.cloned.1.call-done), kind=kOutput, calls=%fused_computation.35 | convolution fusion | flops 2147483648 | bytes 18874368 | tf_op jit(solution)/shard_map/rl,rv->lv/dot_general | solution.py:54
  96.6 98.7 %psum.44 = f32[128]{0:T(128)S(1)} all-reduce(f32[128]{0:T(128)S(1)} %get-tuple-element.13), channel_id=1, replica_groups=mesh['grp'=8,'lm'=16] {'grp','lm'}, use_global_device_ids=true, to_apply=%region_8.0 | all-reduce | flops 128 | bytes 1024 | tf_op jit(solution)/shard_map/psum | solution.py:49
  196.0 17.4 %all-reduce.1 = (f32[2048]{0:T(1024)S(1)}, f32[]{:T(128)}) all-reduce(f32[2048]{0:T(1024)S(1)} %get-tuple-element.11, f32[]{:T(128)} %convert_reduce_fusion), channel_id=1, replica_groups=mesh['grp'=8,'lm'=16] {'grp'}, use_global_device_ids=true, to_apply=%region_4.0 | all-reduce | flops 2049 | bytes 16392 | tf_op jit(solution)/shard_map/psum | solution.py:45
  214.0 3.9 reduce_sum.92
  218.5 11.8 %fusion.2 = f32[4096,128]{1,0:T(8,128)} fusion(bf16[4096,2048]{1,0:T(8,128)(2,1)} %get-tuple-element.12, f32[128]{0:T(128)S(1)} %convolution_bitcast_fusion.1, f32[4096]{0:T(1024)S(1)} %bitcast.25, f32[2048,128]{1,0:T(8,128)S(1)} %reduce_sum.92, f32[128]{0:T(128)S(1)} %psum.44, f32[2048]{0:T(1024)S(1)} %broadcast_divide_fusion.1), kind=kOutput, calls=%fused_computation.8 | convolution fusion | flops 2149318656 | bytes 19948544 | tf_op jit(solution)/shard_map/dot_general | solution.py:65
  230.4 61.9 %reduce-scatter.3.cloned.1.call-done = f32[256,128]{1,0:T(8,128)} async-done(((f32[4096,128]{1,0:T(8,128)}), f32[256,128]{1,0:T(8,128)}) %reduce-scatter.3.cloned.1.call-update) | async-done | bytes 131088 | tf_op jit(solution)/shard_map/reduce_scatter | solution.py:63
  293.4 68.0 %all-reduce = (f32[128]{0:T(128)S(1)}, f32[128]{0:T(128)S(1)}) all-reduce(f32[128]{0:T(128)S(1)} %get-tuple-element.6, f32[128]{0:T(128)S(1)} %get-tuple-element.5), channel_id=1, replica_groups=mesh['grp'=8,'lm'=16] {'grp','lm'}, use_global_device_ids=true, to_apply=%region_11.0 | all-reduce | flops 256 | bytes 2048 | tf_op jit(solution)/shard_map/psum | solution.py:70
  361.4 1.6 multiply_convert_fusion
  363.3 29.2 %all-gather.13.cloned.1.call-done = bf16[4096,128]{1,0:T(8,128)(2,1)} async-done(((bf16[256,128]{1,0:T(8,128)(2,1)}), bf16[4096,128]{1,0:T(8,128)(2,1)}) %all-gather.13.cloned.1.call-update) | async-done | bytes 1048592 | tf_op jit(solution)/shard_map/all_gather | solution.py:78
  392.5 11.7 %fusion.12 = f32[2048,128]{1,0:T(8,128)} fusion(bf16[4096,2048]{1,0:T(8,128)(2,1)} %get-tuple-element.12, bf16[4096,128]{1,0:T(8,128)(2,1)} %all-gather.13.cloned.1.call-done), kind=kOutput, calls=%fused_computation.36 | convolution fusion | flops 2147483648 | bytes 18874368 | tf_op jit(solution)/shard_map/rl,rv->lv/dot_general | solution.py:54
  404.2 108.3 %all-gather.17.cloned.1.call-done = f32[16384,128]{1,0:T(8,128)} async-done(((f32[2048,128]{1,0:T(8,128)}), f32[16384,128]{1,0:T(8,128)}) %all-gather.17.cloned.1.call-update) | async-done | bytes 8388624 | tf_op jit(solution)/shard_map/all_gather | solution.py:10
  512.6 3.9 reduce_sum.97
  517.0 11.8 %fusion.1 = f32[4096,128]{1,0:T(8,128)} fusion(bf16[4096,2048]{1,0:T(8,128)(2,1)} %get-tuple-element.12, f32[128]{0:T(128)S(1)} %convolution_bitcast_fusion, f32[4096]{0:T(1024)S(1)} %bitcast.26, f32[2048,128]{1,0:T(8,128)S(1)} %reduce_sum.97, f32[128]{0:T(128)S(1)} %get-tuple-element.15, f32[2048]{0:T(1024)S(1)} %broadcast_divide_fusion.1), kind=kOutput, calls=%fused_computation.6 | convolution fusion | flops 2149318656 | bytes 19948544 | tf_op jit(solution)/shard_map/dot_general | solution.py:65
  528.8 58.4 %reduce-scatter.5.cloned.1.call-done = f32[256,128]{1,0:T(8,128)} async-done(((f32[4096,128]{1,0:T(8,128)}), f32[256,128]{1,0:T(8,128)}) %reduce-scatter.5.cloned.1.call-update) | async-done | bytes 131088 | tf_op jit(solution)/shard_map/reduce_scatter | solution.py:63
  588.2 68.1 %psum.47 = f32[128]{0:T(128)S(1)} all-reduce(f32[128]{0:T(128)S(1)} %multiply_reduce_fusion.1), channel_id=1, replica_groups=mesh['grp'=8,'lm'=16] {'grp','lm'}, use_global_device_ids=true, to_apply=%region_17.0 | all-reduce | flops 128 | bytes 1024 | tf_op jit(solution)/shard_map/psum | solution.py:70
  656.3 1.6 broadcast_divide_fusion
  (30 shorter events, 5.7 us)
Async XLA Ops:
  6.5 44.1 %all-gather.9.cloned.1.call-start = ((), (), s32[]{:S(2)}) async-start(), calls=%async_computation.2 | async-start | bytes 4456448 | tf_op jit(solution)/shard_map/all_gather | solution.py:37
  9.4 75.4 %all-gather.11.cloned.1.call-start = ((), (), s32[]{:S(2)}) async-start(), calls=%async_computation.3 | async-start | bytes 1114112 | tf_op jit(solution)/shard_map/all_gather | solution.py:50
  11.1 202.9 %all-gather.15.cloned.1.call-start = ((), (), s32[]{:S(2)}) async-start(), calls=%async_computation.7 | async-start | bytes 9437184 | tf_op jit(solution)/shard_map/all_gather | solution.py:10
  96.5 195.8 %reduce-scatter.3.cloned.1.call-start = ((), (), s32[]{:S(2)}) async-start(), calls=%async_computation.4 | async-start | bytes 2228224 | tf_op jit(solution)/shard_map/reduce_scatter | solution.py:63
  218.5 73.8 %copy-start = (f32[256]{0:T(256)S(1)}, f32[256]{0:T(256)}, u32[]{:S(2)}) copy-start(f32[256]{0:T(256)} %param.8) | copy-start | bytes 3076
  230.3 162.1 %all-gather.13.cloned.1.call-start = ((), (), s32[]{:S(2)}) async-start(), calls=%async_computation.5 | async-start | bytes 1114112 | tf_op jit(solution)/shard_map/all_gather | solution.py:78
  363.1 149.5 %all-gather.17.cloned.1.call-start = ((), (), s32[]{:S(2)}) async-start(), calls=%async_computation.8 | async-start | bytes 9437184 | tf_op jit(solution)/shard_map/all_gather | solution.py:10
  404.2 183.0 %reduce-scatter.5.cloned.1.call-start = ((), (), s32[]{:S(2)}) async-start(), calls=%async_computation.6 | async-start | bytes 2228224 | tf_op jit(solution)/shard_map/reduce_scatter | solution.py:63
Sparse Core Ops, SparseCore 0:
  9.5 41.0 all-gather.8
  52.3 32.4 all-gather.10
  96.7 109.5 all-gather.14
  230.5 61.8 reduce-scatter.2
  363.2 29.2 all-gather.12
  404.3 108.1 all-gather.16
  529.0 58.2 reduce-scatter.4
